TPU v7x, 128 devices: a whole 4x4x4 slice. The times are simulated.
128 devices in a mesh: inner: 8 (over z_lo, y), outer: 16 (over x, z_hi, core).
Axes of the slice: x: 4, y: 4, z: 4 (z_hi: 2, z_lo: 2; z = z_hi * 2 + z_lo), core: 2. Of those that a mesh axis runs over, the one named last changes fastest.
Arguments:
- queries: bfloat16 [262144, 256], P(('outer', 'inner')), may hold values from -24 to 24
- keys: bfloat16 [262144, 256], P(('outer', 'inner')), may hold values from -24 to 24
- values: bfloat16 [262144, 256], P(('outer', 'inner')), may hold values from -6 to 6
- offsets_group: int32 [16, 2], replicated, may hold values from 0 to 7
- offsets_global: int32 [2], replicated, may hold values from 0 to 127
- out_weight: bfloat16 [256, 4096], replicated, may hold values from -0.375 to 0.375
Outputs:
- projected: bfloat16 [262144, 4096], P(('outer', 'inner'))
All inputs are finite; a program needn't handle non-finite values.
Results may differ from a plain program's by a relative error of at most 0.0054.
Values may be sent and summed in bfloat16 or wider, within the bound.
A program may use at most 128 MiB of HBM per device.

v0:
```python
import jax
import jax.numpy as jnp
from jax import lax
from jax.sharding import PartitionSpec as P

HD = 128
HEADS = 2


def attend(query, keys_in, values_in, query_pos, key_pos):
    scores = jnp.dot(query, keys_in.T, preferred_element_type=jnp.float32) * HD ** (-0.5)
    scores = jnp.where(key_pos[None, :] <= query_pos[:, None], scores, -jnp.inf)
    top = jnp.max(scores, axis=1)
    expo = jnp.exp(scores - top[:, None])
    denom = jnp.sum(expo, axis=1)
    out = (
        jnp.dot(expo.astype(jnp.bfloat16), values_in, preferred_element_type=jnp.float32)
        / denom[:, None]
    )
    return (out, top + jnp.log(denom))


def select_rows(matrix, head, offset, rate):
    part = matrix[:, head * HD : (head + 1) * HD]
    rows = part.shape[0]
    return lax.dynamic_index_in_dim(part.reshape(rows // rate, rate, HD), offset, 1, False)


def select_heads(matrix, offsets, rate):
    return jnp.concatenate(
        [select_rows(matrix, head, offsets[head], rate) for head in range(HEADS)], axis=1
    )


def blend(acc, lse, out_p, lse_p, offset, rate):
    rows = acc.shape[0]
    acc3 = acc.reshape(rows // rate, rate, HD)
    lse2 = lse.reshape(rows // rate, rate)
    prior = lax.dynamic_index_in_dim(acc3, offset, 1, False)
    prior_lse = lax.dynamic_index_in_dim(lse2, offset, 1, False)
    fresh = jnp.logaddexp(prior_lse, lse_p)
    mixed = prior * jnp.exp(prior_lse - fresh)[:, None] + out_p * jnp.exp(lse_p - fresh)[:, None]
    acc3 = lax.dynamic_update_index_in_dim(acc3, mixed, offset, 1)
    lse2 = lax.dynamic_update_index_in_dim(lse2, fresh, offset, 1)
    return (acc3.reshape(rows, HD), lse2.reshape(rows))


def local_pattern(q_head, k_head, v_head):
    rows = q_head.shape[0]
    block = min(512, rows)
    spots = jnp.arange(rows, dtype=jnp.int32)
    outs = []
    sums = []
    for index in range(rows // block):
        lower = index * block
        upper = lower + block
        out, lse = attend(q_head[lower:upper], k_head, v_head, spots[lower:upper], spots)
        outs.append(out)
        sums.append(lse)
    return (jnp.concatenate(outs, axis=0), jnp.concatenate(sums, axis=0))


def group_gather(sel_gk, sel_gv):
    return (
        lax.all_gather(sel_gk, "inner", axis=0, tiled=True),
        lax.all_gather(sel_gv, "inner", axis=0, tiled=True),
    )


def per_device(queries, keys, values, offsets_group, offsets_global, out_weight):
    n_inner = lax.axis_size("inner")
    n_outer = lax.axis_size("outer")
    rows = queries.shape[0]
    whole_rate = n_inner * n_outer
    segment_offsets = lax.dynamic_index_in_dim(offsets_group, lax.axis_index("outer"), 0, False)
    sel_gk = select_heads(keys, segment_offsets, n_inner)
    sel_gv = select_heads(values, segment_offsets, n_inner)
    sel_k = select_heads(keys, offsets_global, whole_rate)
    sel_v = select_heads(values, offsets_global, whole_rate)
    n_sel = sel_k.shape[0]
    group_k, group_v = group_gather(sel_gk, sel_gv)
    part_k, part_v = (
        lax.all_gather(sel_k, "inner", axis=0, tiled=True),
        lax.all_gather(sel_v, "inner", axis=0, tiled=True),
    )
    whole_k, whole_v = (
        lax.all_gather(part_k, "outer", axis=0, tiled=True),
        lax.all_gather(part_v, "outer", axis=0, tiled=True),
    )
    n_group = rows // n_inner
    group_qpos = lax.axis_index("inner") * n_group + jnp.arange(n_group, dtype=jnp.int32)
    group_kpos = jnp.arange(group_k.shape[0], dtype=jnp.int32)
    device_rank = lax.axis_index("outer") * n_inner + lax.axis_index("inner")
    whole_qpos = device_rank * n_sel + jnp.arange(n_sel, dtype=jnp.int32)
    whole_kpos = jnp.arange(whole_k.shape[0], dtype=jnp.int32)
    heads_out = []
    for head in range(HEADS):
        cols = slice(head * HD, (head + 1) * HD)
        acc, lse = local_pattern(queries[:, cols], keys[:, cols], values[:, cols])
        offset = segment_offsets[head]
        out_p, lse_p = attend(
            select_rows(queries, head, offset, n_inner),
            group_k[:, cols],
            group_v[:, cols],
            group_qpos,
            group_kpos,
        )
        acc, lse = blend(acc, lse, out_p, lse_p, offset, n_inner)
        offset = offsets_global[head]
        out_p, lse_p = attend(
            select_rows(queries, head, offset, whole_rate),
            whole_k[:, cols],
            whole_v[:, cols],
            whole_qpos,
            whole_kpos,
        )
        acc, lse = blend(acc, lse, out_p, lse_p, offset, whole_rate)
        heads_out.append(acc)
    attended = jnp.concatenate(heads_out, axis=1).astype(jnp.bfloat16)
    return jnp.dot(attended, out_weight, preferred_element_type=jnp.float32).astype(jnp.bfloat16)


def solution(mesh):
    in_specs = (
        P(("outer", "inner"), None),
        P(("outer", "inner"), None),
        P(("outer", "inner"), None),
        P(),
        P(),
        P(),
    )
    out_specs = P(("outer", "inner"), None)
    return jax.shard_map(
        per_device, mesh=mesh, in_specs=in_specs, out_specs=out_specs, check_vma=False
    )
```

profile of v0, /device:TPU:38, one launch (start us, length us, event | category | flops | bytes accessed | tf_op | source)
XLA Modules:
  0.0 212.3 jit_solution(2462773332960224643)
XLA Ops:
  6.5 0.9 constant_dynamic-slice_fusion.18
  10.5 2.7 %fusion.143 = (bf16[2048,128]{1,0:T(8,128)(2,1)}, bf16[256,8,128]{2,1,0:T(8,128)(2,1)}, bf16[256,8,128]{2,1,0:T(8,128)(2,1)}, bf16[2048,128]{1,0:T(8,128)(2,1)}) fusion(bf16[2048,256]{1,0:T(8,128)(2,1)} %param.7), kind=kLoop, calls=%fused_computation.223 | loop fusion | bytes 3145728 | tf_op jit(solution)/shard_map/slice | solution.py:99
  14.5 1.5 constant_dynamic-slice_fusion.13
  16.7 1.3 fusion.144
  22.8 0.8 constant_dynamic-slice_fusion.6
  24.2 0.8 constant_dynamic-slice_fusion.5
  25.0 30.2 %all_gather.20 = bf16[128,256]{1,0:T(8,128)(2,1)} all-gather(bf16[16,256]{1,0:T(8,128)(2,1)S(1)} %pad_maximum_fusion.3), channel_id=1, replica_groups=mesh['inner'=8,'outer'=16] {'inner'}, dimensions={0}, use_global_device_ids=true | all-gather | bytes 73728 | tf_op jit(solution)/shard_map/all_gather | solution.py:83
  55.4 30.1 %all_gather.22 = bf16[128,256]{1,0:T(8,128)(2,1)} all-gather(bf16[16,256]{1,0:T(8,128)(2,1)S(1)} %pad_maximum_fusion.4), channel_id=1, replica_groups=mesh['inner'=8,'outer'=16] {'inner'}, dimensions={0}, use_global_device_ids=true | all-gather | bytes 73728 | tf_op jit(solution)/shard_map/all_gather | solution.py:84
  85.5 2.7 %fusion.142 = (bf16[2048,128]{1,0:T(8,128)(2,1)}, bf16[256,8,128]{2,1,0:T(8,128)(2,1)}, bf16[256,8,128]{2,1,0:T(8,128)(2,1)}, bf16[2048,128]{1,0:T(8,128)(2,1)}) fusion(bf16[2048,256]{1,0:T(8,128)(2,1)} %param.6), kind=kLoop, calls=%fused_computation.222 | loop fusion | bytes 3145728 | tf_op jit(solution)/shard_map/slice | solution.py:99
  88.2 2.1 fusion.147
  90.3 0.7 fusion.14
  91.0 0.8 fusion.69
  91.8 0.9 fusion.153
  92.8 0.7 fusion.6
  93.5 1.5 fusion.57
  95.0 1.0 fusion.148
  96.0 0.7 fusion.12
  96.7 1.5 fusion.66
  98.2 0.9 fusion.154
  99.1 0.7 fusion.4
  99.8 1.5 fusion.54
  101.3 0.9 fusion.149
  102.3 0.7 fusion.10
  103.0 1.5 fusion.63
  104.5 1.2 fusion.155
  105.7 0.7 fusion.2
  106.4 1.5 fusion.51
  107.9 1.0 fusion.150
  108.9 0.7 fusion.8
  109.6 1.5 fusion.60
  111.1 1.0 fusion.156
  112.1 0.7 fusion
  112.8 1.5 fusion.48
  115.4 1.4 constant_dynamic-slice_fusion.9
  116.8 1.4 constant_dynamic-slice_fusion
  118.4 0.7 copy.56
  120.8 0.7 copy.54
  121.6 0.7 copy.64
  122.2 1.2 maximum_bitcast_fusion.1
  123.4 1.0 copy-done.4
  125.3 1.3 maximum_bitcast_fusion
  126.6 2.1 %constant_dynamic-slice_fusion.2 = (bf16[256,1,128]{2,1,0:T(2,128)(2,1)}, bf16[256,1,128]{2,1,0:T(2,128)(2,1)S(1)}) fusion(bf16[256,8,128]{2,1,0:T(8,128)(2,1)} %get-tuple-element.15, s32[]{:T(128)S(6)} %select_n.114, bf16[256,8,128]{2,1,0:T(8,128)(2,1)} %get-tuple-element.14, s32[]{:T(128)S(6)} %select_n.113), kind=kLoop, calls=%fused_computation.150 | loop fusion | bytes 262152 | tf_op jit(solution)/shard_map/jit(dynamic_index_in_dim)/dynamic_slice | solution.py:26
  128.8 0.8 pad_maximum_fusion.5
  129.5 0.8 pad_maximum_fusion.2
  130.3 1.7 fusion.151
  132.0 1.3 copy-done.3
  136.1 1.6 fusion.157
  137.8 1.3 copy-done.2
  141.0 2.2 %fusion.73 = f32[256,128]{1,0:T(8,128)S(1)} fusion(f32[256,2048]{1,0:T(8,128)} %copy-done.3, f32[256]{0:T(256)} %copy-done.9, bf16[2048,256]{1,0:T(8,128)(2,1)} %all-gather.7.cloned.1.call-done, f32[256,128]{1,0:T(8,128)S(1)} %bitcast.114, f32[256]{0:T(256)} %bitcast.133, f32[256]{0:T(256)} %copy-done.10, f32[256]{0:T(256)} %bitcast.135), kind=kOutput, calls=%fused_computation.78 | convolution fusion | flops 135397376 | bytes 2887680 | tf_op jit(solution)/shard_map/dot_general | solution.py:17
  143.2 4.7 %dynamic_update_slice.24 = f32[256,8,128]{2,1,0:T(8,128)} dynamic-update-slice(f32[256,8,128]{2,1,0:T(8,128)} %copy-done.4, f32[256,1,128]{2,1,0:T(1,128)S(1)} %bitcast.116, s32[]{:T(128)} %constant.91.clone.1, s32[]{:T(128)S(6)} %select_n.114, s32[]{:T(128)} %constant.91.clone.1) | dynamic-update-slice | bytes 262148 | tf_op jit(solution)/shard_map/jit(dynamic_update_index_in_dim)/dynamic_update_slice | solution.py:43
  147.9 0.7 subtract_exponential_fusion.15
  149.1 0.7 subtract_exponential_fusion.14
  149.8 2.2 %fusion.75 = f32[256,128]{1,0:T(8,128)S(1)} fusion(f32[256,2048]{1,0:T(8,128)} %copy-done.2, f32[256]{0:T(256)} %copy-done.7, bf16[2048,256]{1,0:T(8,128)(2,1)} %all-gather.7.cloned.1.call-done, f32[256,128]{1,0:T(8,128)S(1)} %bitcast.113, f32[256]{0:T(256)S(1)} %bitcast.134, f32[256]{0:T(256)} %copy-done.8, f32[256]{0:T(256)S(1)} %bitcast.136), kind=kOutput, calls=%fused_computation.81 | convolution fusion | flops 135397376 | bytes 2887680 | tf_op jit(solution)/shard_map/dot_general | solution.py:17
  152.0 2.8 %dynamic_update_slice.21 = f32[256,8,128]{2,1,0:T(8,128)S(1)} dynamic-update-slice(f32[256,8,128]{2,1,0:T(8,128)S(1)} %maximum_bitcast_fusion, f32[256,1,128]{2,1,0:T(1,128)S(1)} %bitcast.115, s32[]{:T(128)} %constant.91.clone.1, s32[]{:T(128)S(6)} %select_n.113, s32[]{:T(128)} %constant.91.clone.1) | dynamic-update-slice | bytes 262148 | tf_op jit(solution)/shard_map/jit(dynamic_update_index_in_dim)/dynamic_update_slice | solution.py:43
  154.8 0.9 constant_dynamic-slice_fusion.1
  155.7 1.4 fusion.152
  157.4 1.4 fusion.158
  159.4 29.3 %all-gather.11.cloned.1.call-done = bf16[2048,256]{1,0:T(8,128)(2,1)} async-done(((bf16[128,256]{1,0:T(8,128)(2,1)}), bf16[2048,256]{1,0:T(8,128)(2,1)}) %all-gather.11.cloned.1.call-update) | async-done | bytes 1048592 | tf_op jit(solution)/shard_map/all_gather | solution.py:88
  188.7 1.3 fusion.77
  190.0 1.5 dynamic_update_slice.26
  191.5 2.1 convert.9
  193.8 1.3 fusion.79
  195.2 0.9 convert.8
  196.1 9.7 %convolution_convert_fusion = bf16[2048,4096]{1,0:T(8,128)(2,1)} fusion(bf16[256,4096]{1,0:T(8,128)(2,1)S(1)} %copy-done, bf16[2048,128]{1,0:T(8,128)(2,1)} %bitcast.105, bf16[2048,128]{1,0:T(8,128)(2,1)} %bitcast.106), kind=kOutput, calls=%fused_computation | convolution fusion | flops 4305453056 | bytes 19922944 | tf_op jit(solution)/shard_map/dot_general | solution.py:120
  (104 shorter events, 13.5 us)
Async XLA Ops:
  6.5 189.5 %copy-start = (bf16[256,4096]{1,0:T(8,128)(2,1)S(1)}, bf16[256,4096]{1,0:T(8,128)(2,1)}, u32[]{:S(2)}) copy-start(bf16[256,4096]{1,0:T(8,128)(2,1)} %param.11) | copy-start | bytes 6291460
  6.5 10.2 %copy-start.1 = (bf16[2048,256]{1,0:T(8,128)(2,1)S(1)}, bf16[2048,256]{1,0:T(8,128)(2,1)}, u32[]{:S(2)}) copy-start(bf16[2048,256]{1,0:T(8,128)(2,1)} %param.8) | copy-start | bytes 3145732
  6.5 123.8 %all-gather.5.cloned.1.call-start = ((), (), s32[]{:S(2)}) async-start(), calls=%async_computation | async-start | bytes 1179648 | tf_op jit(solution)/shard_map/all_gather | solution.py:65
  10.5 8.5 %copy-start.13 = (s32[2]{0:T(128)S(1)}, s32[2]{0:T(128)}, u32[]{:S(2)}) copy-start(s32[2]{0:T(128)} %param.10) | copy-start | bytes 28
  16.7 124.3 %all-gather.7.cloned.1.call-start = ((), (), s32[]{:S(2)}) async-start(), calls=%async_computation.1 | async-start | bytes 1179648 | tf_op jit(solution)/shard_map/all_gather | solution.py:66
  19.0 136.7 %all-gather.9.cloned.1.call-start = ((), (), s32[]{:S(2)}) async-start(), calls=%async_computation.2 | async-start | bytes 1114112 | tf_op jit(solution)/shard_map/all_gather | solution.py:87
  55.3 133.4 %all-gather.11.cloned.1.call-start = ((), (), s32[]{:S(2)}) async-start(), calls=%async_computation.3 | async-start | bytes 1114112 | tf_op jit(solution)/shard_map/all_gather | solution.py:88
  90.3 1.5 copy-start.5
  90.3 1.5 copy-start.6
  123.4 1.0 copy-start.4
  132.0 1.3 copy-start.3
  132.0 2.4 %copy-start.9 = (f32[256]{0:T(256)}, f32[256]{0:T(256)S(1)}, u32[]{:S(2)}) copy-start(f32[256]{0:T(256)S(1)} %get-tuple-element.37) | copy-start | bytes 3076
  133.7 0.6 copy-start.10
  134.3 0.5 copy-start.11
  137.8 1.4 copy-start.2
  137.8 1.8 copy-start.7
  139.6 0.6 copy-start.8
  147.9 9.6 %copy-start.12 = (bf16[16,1,128]{2,1,0:T(2,128)(2,1)S(1)}, bf16[16,1,128]{2,1,0:T(2,128)(2,1)}, u32[]{:S(2)}) copy-start(bf16[16,1,128]{2,1,0:T(2,128)(2,1)} %constant_dynamic-slice_fusion.9) | copy-start | bytes 12292
  147.9 9.6 %copy-start.14 = (s32[16]{0:T(128)S(1)}, s32[16]{0:T(128)}, u32[]{:S(2)}) copy-start(s32[16]{0:T(128)} %iota_add_fusion.5) | copy-start | bytes 196
Sparse Core Ops, SparseCore 0:
  16.8 40.2 all-gather.4
  58.7 37.6 all-gather.6
  98.8 43.7 all-gather.8
  144.9 43.7 all-gather.10
where the time goes:
time: 217 us; the launch traced here: 212 us
  blocking collectives  60.3 us (28%)
  matrix products  43.1 us (20%)
  local copies, waits for them, and re-layouts  38.2 us (18%)
  waiting for transfers between devices  29.4 us (14%)
  between operations  21.1 us (10%)
  other arithmetic  20.1 us (9%)
    all_gather x1, blocking collectives, per_device(): lax.all_gather(sel_k, 'inner', axis=0, tiled=True)  30.2 us
    all_gather x1, blocking collectives, per_device(): lax.all_gather(sel_v, 'inner', axis=0, tiled=True)  30.1 us
    all_gather x1, waiting for transfers between devices, per_device(): lax.all_gather(part_v, 'outer', axis=0, tiled=True)  29.3 us
    dot_general x12, matrix products, attend(): jnp.dot(expo.astype(jnp.bfloat16), values_in, preferred_element_type=jnp....  18.3 us
    dot_general x12, matrix products, attend(): jnp.dot(query, keys_in.T, preferred_element_type=jnp.float32) * HD ** (-0.5)  15 us
    dot_general x1, matrix products, per_device(): jnp.dot(attended, out_weight, preferred_element_type=jnp.float32)  9.7 us
    dynamic_update_slice x4, local copies, waits for them, and re-layouts, blend(): acc3 = lax.dynamic_update_index_in_dim(acc3, mixed, offset, 1)  9.05 us
    dynamic_slice x7, local copies, waits for them, and re-layouts, select_rows(): lax.dynamic_index_in_dim(part.reshape(rows // rate, rate, HD), offset, 1,...  8.23 us
  transfers between devices with their start and end apart: 4, of which 1 were waited for; matrix products, arithmetic and copies ran while one was open for 34% of the time, Pallas kernels for 0%

commit v1 on v0

v1 whole, which is shorter than its diff:
```python
import functools

import jax
import jax.numpy as jnp
from jax import lax
from jax.experimental import pallas as pl
from jax.experimental.pallas import tpu as pltpu
from jax.sharding import PartitionSpec as P

HD = 128
HEADS = 2
ROWS = 2048
RING = 4
PLANES = 2
GROUP = RING * PLANES
GROUPS = 16
SEL = ROWS // GROUP
WHOLE = ROWS // (GROUP * GROUPS)
BQ = 256
BLOCKS = ROWS // BQ
SCALE = HD**-0.5 * 1.4426950408889634
NEG = -1e30
F32 = jnp.float32
BF16 = jnp.bfloat16


def iota(shape, dim):
    return lax.broadcasted_iota(jnp.int32, shape, dim)


def cols(head):
    return slice(head * HD, (head + 1) * HD)


def dot_t(a, b):
    return lax.dot_general(a, b, (((1,), (1,)), ((), ())), preferred_element_type=F32)


def dot(a, b):
    return jnp.dot(a, b, preferred_element_type=F32)


def wide(column, rows):
    return jnp.broadcast_to(column, (rows, HD))


def finish(scores, values):
    rows = scores.shape[0]
    top = jnp.max(scores, axis=1, keepdims=True)
    expo = jnp.exp2((scores - top) * SCALE)
    total = jnp.sum(expo, axis=1, keepdims=True)
    out = dot(expo.astype(BF16), values) / total
    return out, wide(top * SCALE + jnp.log2(total), rows)


def local_tile(q_ref, k_ref, vx_ref, block, head):
    low = block * BQ
    high = low + BQ
    scores = dot_t(q_ref[low:high, cols(head)], k_ref[0:high, cols(head)])
    diag = jnp.where(iota((BQ, BQ), 1) <= iota((BQ, BQ), 0), scores[:, low:], NEG)
    scores = diag if block == 0 else jnp.concatenate([scores[:, :low], diag], axis=1)
    top = jnp.max(scores, axis=1, keepdims=True)
    expo = jnp.exp2((scores - top) * SCALE)
    out = dot(expo.astype(BF16), vx_ref[0:high, head * 2 * HD : (head + 1) * 2 * HD])
    total = out[:, HD:]
    return out[:, :HD] / total, top * SCALE + jnp.log2(total)


def merge(out0, lse0, out1, lse1, out2, lse2, offset1, offset2):
    spots = iota((BQ, HD), 0)
    n1 = BQ // GROUP
    n2 = BQ // (GROUP * GROUPS)

    def spread(part, count):
        return jnp.broadcast_to(part[:, None, :], (count, BQ // count, HD)).reshape(BQ, HD)

    e1 = jnp.where(lax.rem(spots, GROUP) == offset1, spread(lse1, n1), NEG)
    e2 = jnp.where(lax.rem(spots, GROUP * GROUPS) == offset2, spread(lse2, n2), NEG)
    top = jnp.maximum(jnp.maximum(lse0, e1), e2)
    w0 = jnp.exp2(lse0 - top)
    w1 = jnp.exp2(e1 - top)
    w2 = jnp.exp2(e2 - top)
    mixed = w0 * out0 + w1 * spread(out1, n1) + w2 * spread(out2, n2)
    return (mixed / (w0 + w1 + w2)).astype(BF16)


def attention_kernel(
    offg_ref, offw_ref, q_ref, k_ref, v_ref, att_ref,
    vx, out0, lse0, out1, lse1, out2, lse2,
    gk, gv, gq, gqp, gop, gor, gsp, gsr,
    nkv, nq, no_out, no_in,
    send, recv, wq_send, wq_recv, wo_send, wo_recv,
):
    outer = lax.axis_index("outer")
    inner = lax.axis_index("inner")
    plane = inner // RING
    y = inner % RING
    left_y = (y + RING - 1) % RING
    right_y = (y + 1) % RING
    left = plane * RING + left_y
    right = plane * RING + right_y
    across = (1 - plane) * RING + y

    barrier = pltpu.get_barrier_semaphore()
    for peer in (left, right, across):
        pl.semaphore_signal(barrier, inc=1, device_id={"inner": peer}, device_id_type=pl.DeviceIdType.MESH)

    def greet(step, carry):
        pl.semaphore_signal(
            barrier, inc=1, device_id={"outer": (outer + step) % GROUPS}, device_id_type=pl.DeviceIdType.MESH
        )
        return carry

    lax.fori_loop(1, GROUPS, greet, 0)

    def remote(src, dst, index, axis, peer):
        return pltpu.make_async_remote_copy(
            src_ref=src, dst_ref=dst, send_sem=send.at[index], recv_sem=recv.at[index],
            device_id={axis: peer}, device_id_type=pl.DeviceIdType.MESH,
        )

    offs1 = [offg_ref[outer, head] for head in range(HEADS)]
    offs2 = [offw_ref[head] for head in range(HEADS)]
    n1 = BQ // GROUP
    pick1 = [
        (iota((n1, BQ), 1) == iota((n1, BQ), 0) * GROUP + offs1[head]).astype(F32).astype(BF16)
        for head in range(HEADS)
    ]
    own1 = pl.multiple_of(y * SEL, SEL)
    own2 = pl.multiple_of(inner * WHOLE, WHOLE)
    whole = [[jnp.zeros((WHOLE, HD), F32) for _ in range(HEADS)] for _ in range(3)]
    for block in range(BLOCKS):
        low = block * BQ
        pick2 = [
            (iota((WHOLE, BQ), 1) + low == iota((WHOLE, BQ), 0) * (GROUP * GROUPS) + offs2[head])
            .astype(F32).astype(BF16)
            for head in range(HEADS)
        ]
        pick = jnp.concatenate(pick1 + pick2, axis=0)
        for index, ref in enumerate((k_ref, v_ref, q_ref)):
            got = dot(pick, ref[low : low + BQ, :])
            for head in range(HEADS):
                rows1 = got[head * n1 : (head + 1) * n1, cols(head)].astype(BF16)
                if index == 2:
                    gq[head, block * n1 : (block + 1) * n1, :] = rows1
                else:
                    (gk, gv)[index][head, pl.ds(own1 + block * n1, n1), :] = rows1
                base = HEADS * n1 + head * WHOLE
                whole[index][head] += got[base : base + WHOLE, cols(head)]
    for head in range(HEADS):
        nkv[pl.ds(own2, WHOLE), cols(head)] = whole[0][head].astype(BF16)
        nkv[pl.ds(own2, WHOLE), cols(HEADS + head)] = whole[1][head].astype(BF16)
        nq[pl.ds(pl.multiple_of(outer * WHOLE, WHOLE), WHOLE), cols(head)] = whole[2][head].astype(BF16)

    pl.semaphore_wait(barrier, 3 + GROUPS - 1)

    def whole_slot(index):
        return pl.ds(pl.multiple_of(index * WHOLE, WHOLE), WHOLE)

    mine = nkv.at[whole_slot(inner)]
    nkv_right = remote(mine, mine, 0, "inner", right)
    nkv_left = remote(mine, mine, 1, "inner", left)
    from_left = nkv.at[whole_slot(left), 0 : HEADS * HD]
    from_right = nkv.at[whole_slot(right), HEADS * HD : 2 * HEADS * HD]
    nkv_relay_right = remote(from_left, from_left, 2, "inner", right)
    nkv_relay_left = remote(from_right, from_right, 3, "inner", left)
    half = pl.ds(pl.multiple_of(plane * RING * WHOLE, RING * WHOLE), RING * WHOLE)
    nkv_across = remote(nkv.at[half], nkv.at[half], 4, "inner", across)

    def query_copy(peer, slot):
        rows = whole_slot(slot)
        return pltpu.make_async_remote_copy(
            src_ref=nq.at[whole_slot(outer)], dst_ref=nq.at[rows],
            send_sem=wq_send.at[peer], recv_sem=wq_recv.at[slot],
            device_id={"outer": peer}, device_id_type=pl.DeviceIdType.MESH,
        )

    def result_copy(peer, slot):
        return pltpu.make_async_remote_copy(
            src_ref=no_out.at[whole_slot(peer)], dst_ref=no_in.at[whole_slot(slot)],
            send_sem=wo_send.at[peer], recv_sem=wo_recv.at[slot],
            device_id={"outer": peer}, device_id_type=pl.DeviceIdType.MESH,
        )

    def each_peer(act):
        def body(step, carry):
            act((outer + step) % GROUPS)
            return carry

        lax.fori_loop(1, GROUPS, body, 0)

    def ring_copy(buffer, head, slot_y, index, peer):
        part = buffer.at[head, pl.ds(pl.multiple_of(slot_y * SEL, SEL), SEL)]
        return remote(part, part, index, "inner", peer)

    ring = []
    for head in range(HEADS):
        base = 5 + head * 9
        ring.append(
            dict(
                k_right=ring_copy(gk, head, y, base, right),
                v_right=ring_copy(gv, head, y, base + 1, right),
                v_left=ring_copy(gv, head, y, base + 2, left),
                k_left=ring_copy(gk, head, y, base + 3, left),
                relay_right=ring_copy(gk, head, left_y, base + 4, right),
                relay_left=ring_copy(gv, head, right_y, base + 5, left),
                q=remote(gq.at[head], gqp.at[head], base + 6, "inner", across),
                o=remote(gop.at[head], gor.at[head], base + 7, "inner", across),
                s=remote(gsp.at[head], gsr.at[head], base + 8, "inner", across),
            )
        )

    def start(*copies):
        for copy in copies:
            copy.start()

    def arrived(*copies):
        for copy in copies:
            copy.wait_recv()

    def own_sends(head):
        c = ring[head]
        start(c["k_right"], c["v_left"], c["v_right"], c["k_left"])

    start(nkv_right, nkv_left)
    own_sends(0)
    each_peer(lambda peer: query_copy(peer, outer).start())
    start(ring[0]["q"], ring[1]["q"])

    for head in range(HEADS):
        vx[:, 2 * head * HD : (2 * head + 1) * HD] = v_ref[:, cols(head)]
        vx[:, (2 * head + 1) * HD : (2 * head + 2) * HD] = jnp.ones((ROWS, HD), BF16)

    def local(block):
        for head in range(HEADS):
            out, lse = local_tile(q_ref, k_ref, vx, block, head)
            out0[block * BQ : (block + 1) * BQ, cols(head)] = out
            lse0[block * BQ : (block + 1) * BQ, cols(head)] = lse

    def group_across(head):
        out, lse = finish(dot_t(gqp[head], gk[head]), gv[head])
        gop[head] = out.astype(BF16)
        gsp[head] = lse.T[0:8, :]
        start(ring[head]["o"], ring[head]["s"])

    def group_own(head):
        scores = dot_t(gq[head], gk[head])
        shape = (SEL, RING * SEL)
        out, lse = finish(jnp.where(iota(shape, 1) <= iota(shape, 0) + y * SEL, scores, NEG), gv[head])
        out1[:, cols(head)] = out
        lse1[:, cols(head)] = lse

    def whole_all():
        rows = GROUPS * WHOLE
        keys = GROUP * WHOLE
        shape = (rows, keys)
        row = iota(shape, 0)
        query_pos = (row // WHOLE) * keys + inner * WHOLE + row % WHOLE
        allowed = iota(shape, 1) + outer * keys <= query_pos
        lane = iota((rows, HD), 1)
        stats = jnp.zeros((rows, HD), F32)
        for head in range(HEADS):
            scores = dot_t(nq[:, cols(head)], nkv[:, cols(head)])
            out, lse = finish(jnp.where(allowed, scores, NEG), nkv[:, cols(HEADS + head)])
            no_out[:, cols(head)] = out.astype(BF16)
            for part in range(3):
                term = lse.astype(BF16).astype(F32)
                lse = lse - term
                stats = jnp.where(lane // 16 == 3 * head + part, term, stats)
        no_out[:, cols(HEADS)] = stats.astype(BF16)
        own = whole_slot(outer)
        no_in[own, :] = no_out[own, :]

    local(7)
    arrived(nkv_right, nkv_left)
    start(nkv_relay_right, nkv_relay_left)
    arrived(ring[0]["k_right"], ring[0]["v_left"])
    start(ring[0]["relay_right"], ring[0]["relay_left"])
    own_sends(1)
    local(6)
    arrived(nkv_relay_right, nkv_relay_left)
    start(nkv_across)
    local(5)
    arrived(nkv_across)
    each_peer(lambda peer: query_copy(peer, peer).wait_recv())
    whole_all()
    each_peer(lambda peer: result_copy(peer, outer).start())
    arrived(ring[0]["v_right"], ring[0]["k_left"], ring[0]["relay_right"], ring[0]["relay_left"], ring[0]["q"])
    group_across(0)
    arrived(ring[1]["k_right"], ring[1]["v_left"])
    start(ring[1]["relay_right"], ring[1]["relay_left"])
    group_own(0)
    local(4)
    local(3)
    arrived(ring[1]["v_right"], ring[1]["k_left"], ring[1]["relay_right"], ring[1]["relay_left"], ring[1]["q"])
    group_across(1)
    group_own(1)
    local(2)
    local(1)
    local(0)

    each_peer(lambda peer: result_copy(peer, peer).wait_recv())
    for head in range(HEADS):
        parts = no_in[:, cols(head)].astype(F32).reshape(GROUPS, WHOLE, HD)
        stats = no_in[:, cols(HEADS)].astype(F32)
        lane = 48 * head
        lse = stats[:, lane : lane + 1] + stats[:, lane + 16 : lane + 17] + stats[:, lane + 32 : lane + 33]
        lse = wide(lse, GROUPS * WHOLE).reshape(GROUPS, WHOLE, HD)
        top = jnp.max(lse, axis=0)
        weight = jnp.exp2(lse - top[None])
        total = jnp.sum(weight, axis=0)
        out2[:, cols(head)] = jnp.sum(weight * parts, axis=0) / total
        lse2[:, cols(head)] = top + jnp.log2(total)

    for head in range(HEADS):
        arrived(ring[head]["o"], ring[head]["s"])
        there = jnp.broadcast_to(gsr[head, 0:1, :], (HD, SEL)).T
        there = jnp.where(plane == 1, there, NEG)
        here = lse1[:, cols(head)]
        top = jnp.maximum(here, there)
        w_here = jnp.exp2(here - top)
        w_there = jnp.exp2(there - top)
        total = w_here + w_there
        out1[:, cols(head)] = (w_here * out1[:, cols(head)] + w_there * gor[head].astype(F32)) / total
        lse1[:, cols(head)] = top + jnp.log2(total)

    n2 = BQ // (GROUP * GROUPS)
    for block in range(BLOCKS):
        rows = slice(block * BQ, (block + 1) * BQ)
        rows1 = slice(block * n1, (block + 1) * n1)
        rows2 = slice(block * n2, (block + 1) * n2)
        for head in range(HEADS):
            c = cols(head)
            att_ref[rows, c] = merge(
                out0[rows, c], lse0[rows, c], out1[rows1, c], lse1[rows1, c], out2[rows2, c], lse2[rows2, c],
                offs1[head], offs2[head],
            )

    for copy in (nkv_right, nkv_left, nkv_relay_right, nkv_relay_left, nkv_across):
        copy.wait_send()
    for head in range(HEADS):
        for copy in ring[head].values():
            copy.wait_send()
    each_peer(lambda peer: query_copy(peer, outer).wait_send())
    each_peer(lambda peer: result_copy(peer, outer).wait_send())


def attention(queries, keys, values, offsets_group, offsets_global):
    vmem = pl.BlockSpec(memory_space=pltpu.VMEM)
    smem = pl.BlockSpec(memory_space=pltpu.SMEM)
    dma = pltpu.SemaphoreType.DMA
    return pl.pallas_call(
        attention_kernel,
        out_shape=jax.ShapeDtypeStruct((ROWS, HEADS * HD), BF16),
        in_specs=[smem, smem, vmem, vmem, vmem],
        out_specs=vmem,
        scratch_shapes=[
            pltpu.VMEM((ROWS, 2 * HEADS * HD), BF16),
            pltpu.VMEM((ROWS, HEADS * HD), F32),
            pltpu.VMEM((ROWS, HEADS * HD), F32),
            pltpu.VMEM((SEL, HEADS * HD), F32),
            pltpu.VMEM((SEL, HEADS * HD), F32),
            pltpu.VMEM((WHOLE, HEADS * HD), F32),
            pltpu.VMEM((WHOLE, HEADS * HD), F32),
            pltpu.VMEM((HEADS, RING * SEL, HD), BF16),
            pltpu.VMEM((HEADS, RING * SEL, HD), BF16),
            pltpu.VMEM((HEADS, SEL, HD), BF16),
            pltpu.VMEM((HEADS, SEL, HD), BF16),
            pltpu.VMEM((HEADS, SEL, HD), BF16),
            pltpu.VMEM((HEADS, SEL, HD), BF16),
            pltpu.VMEM((HEADS, 8, SEL), F32),
            pltpu.VMEM((HEADS, 8, SEL), F32),
            pltpu.VMEM((GROUP * WHOLE, 2 * HEADS * HD), BF16),
            pltpu.VMEM((GROUPS * WHOLE, HEADS * HD), BF16),
            pltpu.VMEM((GROUPS * WHOLE, (HEADS + 1) * HD), BF16),
            pltpu.VMEM((GROUPS * WHOLE, (HEADS + 1) * HD), BF16),
            dma((23,)),
            dma((23,)),
            dma((GROUPS,)),
            dma((GROUPS,)),
            dma((GROUPS,)),
            dma((GROUPS,)),
        ],
        compiler_params=pltpu.CompilerParams(
            collective_id=0, has_side_effects=True, vmem_limit_bytes=40 * 2**20
        ),
        cost_estimate=pl.CostEstimate(flops=5 * 10**9, bytes_accessed=4 * 2**20, transcendentals=6 * 10**6),
        name="attention",
    )(offsets_group, offsets_global, queries, keys, values)


CHUNK = 256
CHUNKS = ROWS // CHUNK
SLOTS = 4


def project_kernel(a_ref, w_ref, o_ref, buf, sem):
    def copy(chunk):
        return pltpu.make_async_copy(
            buf.at[chunk % SLOTS], o_ref.at[pl.ds(chunk * CHUNK, CHUNK)], sem.at[chunk % SLOTS]
        )

    for chunk in range(CHUNKS):
        if chunk >= SLOTS:
            copy(chunk - SLOTS).wait()
        buf[chunk % SLOTS] = dot(a_ref[chunk * CHUNK : (chunk + 1) * CHUNK, :], w_ref[...]).astype(BF16)
        copy(chunk).start()
    for chunk in range(CHUNKS - SLOTS, CHUNKS):
        copy(chunk).wait()


def project(attended, weight):
    vmem = pl.BlockSpec(memory_space=pltpu.VMEM)
    width = weight.shape[1]
    return pl.pallas_call(
        project_kernel,
        out_shape=jax.ShapeDtypeStruct((ROWS, width), BF16),
        in_specs=[vmem, vmem],
        out_specs=pl.BlockSpec(memory_space=pl.ANY),
        scratch_shapes=[pltpu.VMEM((SLOTS, CHUNK, width), BF16), pltpu.SemaphoreType.DMA((SLOTS,))],
        compiler_params=pltpu.CompilerParams(vmem_limit_bytes=40 * 2**20),
        cost_estimate=pl.CostEstimate(flops=43 * 10**8, bytes_accessed=19 * 2**20, transcendentals=0),
        name="project",
    )(attended, weight)


def per_device(queries, keys, values, offsets_group, offsets_global, out_weight):
    attended = attention(queries, keys, values, offsets_group, offsets_global)
    return project(attended, out_weight)


def solution(mesh):
    rows = P(("outer", "inner"), None)
    return jax.shard_map(
        per_device, mesh=mesh, in_specs=(rows, rows, rows, P(), P(), P()), out_specs=rows, check_vma=False
    )
```

time: 217 us -> 44.4 us (0.20)
  the two profiles are of different devices: /device:TPU:38 before, /device:TPU:0 now
where the time goes in v1:
time: 44.4 us; the launch traced here: 44.2 us
  Pallas kernels  38.8 us (87%)
  local copies, waits for them, and re-layouts  5.24 us (12%)
    pallas_call x1, Pallas kernels, attention(): pl.pallas_call(attention_kernel, out_shape=jax.ShapeDtypeStruct((ROWS, HE...  32.2 us
    pallas_call x1, Pallas kernels, project(): pl.pallas_call(project_kernel, out_shape=jax.ShapeDtypeStruct((ROWS, widt...  6.62 us
    unnamed x11, local copies, waits for them, and re-layouts  5.24 us

profile of v1, /device:TPU:0, one launch (start us, length us, event | category | flops | bytes accessed | tf_op | source)
XLA Modules:
  0.0 44.2 jit_solution(1265006407952805095)
XLA Ops:
  0.0 0.0 copy-start
  0.0 0.9 %copy.7.offg_ref = s32[16,2]{1,0:T(8,128)S(1)} copy(s32[16,2]{0,1:T(2,128)} %param.9) | data formatting | bytes 256 | tf_op args[3]
  0.9 0.0 copy-start.1
  0.9 1.2 %copy-done.1 = bf16[2048,256]{1,0:T(8,128)(2,1)S(1)} copy-done((bf16[2048,256]{1,0:T(8,128)(2,1)S(1)}, bf16[2048,256]{1,0:T(8,128)(2,1)}, u32[]{:S(2)}) %copy-start.1) | copy-done | bytes 1048600
  2.1 0.0 copy-start.2
  2.1 1.2 %copy-done.2 = bf16[2048,256]{1,0:T(8,128)(2,1)S(1)} copy-done((bf16[2048,256]{1,0:T(8,128)(2,1)S(1)}, bf16[2048,256]{1,0:T(8,128)(2,1)}, u32[]{:S(2)}) %copy-start.2) | copy-done | bytes 1048600
  3.4 0.0 copy-start.3
  3.4 1.2 %copy-done.3 = bf16[2048,256]{1,0:T(8,128)(2,1)S(1)} copy-done((bf16[2048,256]{1,0:T(8,128)(2,1)S(1)}, bf16[2048,256]{1,0:T(8,128)(2,1)}, u32[]{:S(2)}) %copy-start.3) | copy-done | bytes 1048600
  4.6 0.0 copy-start.4
  4.6 0.7 %copy-done.4 = s32[2]{0:T(128)S(1)} copy-done((s32[2]{0:T(128)S(1)}, s32[2]{0:T(128)}, u32[]{:S(2)}) %copy-start.4) | copy-done | bytes 32
  5.2 32.2 %attention.1.a_ref = bf16[2048,256]{1,0:T(8,128)(2,1)S(1)} custom-call(s32[16,2]{1,0:T(8,128)S(1)} %copy.7.offg_ref, s32[2]{0:T(128)S(1)} %copy-done.4, bf16[2048,256]{1,0:T(8,128)(2,1)S(1)} %copy-done.1, bf16[2048,256]{1,0:T(8,128)(2,1)S(1)} %copy-done.2, bf16[2048,256]{1,0:T(8,128)(2,1)S(1)} %copy-done.3), custom_call_target="tpu_custom_call" | custom-call | flops 5000000000 | bytes 4194304 | tf_op jit(solution)/shard_map/attention/pallas_call | solution.py:352
  37.4 0.0 copy-done
  37.4 6.6 %project.1 = bf16[2048,4096]{1,0:T(8,128)(2,1)} custom-call(bf16[2048,256]{1,0:T(8,128)(2,1)S(1)} %attention.1.a_ref, bf16[256,4096]{1,0:T(8,128)(2,1)S(1)} %copy-done), custom_call_target="tpu_custom_call" | custom-call | flops 4300000256 | bytes 19922944 | tf_op jit(solution)/shard_map/project/pallas_call | solution.py:415
Async XLA Ops:
  0.0 37.4 %copy-start = (bf16[256,4096]{1,0:T(8,128)(2,1)S(1)}, bf16[256,4096]{1,0:T(8,128)(2,1)}, u32[]{:S(2)}) copy-start(bf16[256,4096]{1,0:T(8,128)(2,1)} %w_ref.1) | copy-start | bytes 6291460
  0.9 1.2 %copy-start.1 = (bf16[2048,256]{1,0:T(8,128)(2,1)S(1)}, bf16[2048,256]{1,0:T(8,128)(2,1)}, u32[]{:S(2)}) copy-start(bf16[2048,256]{1,0:T(8,128)(2,1)} %q_ref.1) | copy-start | bytes 3145732
  2.1 1.2 %copy-start.2 = (bf16[2048,256]{1,0:T(8,128)(2,1)S(1)}, bf16[2048,256]{1,0:T(8,128)(2,1)}, u32[]{:S(2)}) copy-start(bf16[2048,256]{1,0:T(8,128)(2,1)} %k_ref.1) | copy-start | bytes 3145732
  3.4 1.2 %copy-start.3 = (bf16[2048,256]{1,0:T(8,128)(2,1)S(1)}, bf16[2048,256]{1,0:T(8,128)(2,1)}, u32[]{:S(2)}) copy-start(bf16[2048,256]{1,0:T(8,128)(2,1)} %v_ref.1) | copy-start | bytes 3145732
  4.6 0.7 %copy-start.4 = (s32[2]{0:T(128)S(1)}, s32[2]{0:T(128)}, u32[]{:S(2)}) copy-start(s32[2]{0:T(128)} %offw_ref.1) | copy-start | bytes 28

commit v2 on v0

v2 whole, which is shorter than its diff:
```python
import functools

import jax
import jax.numpy as jnp
from jax import lax
from jax.experimental import pallas as pl
from jax.experimental.pallas import tpu as pltpu
from jax.sharding import PartitionSpec as P

HD = 128
HEADS = 2
ROWS = 2048
RING = 4
PLANES = 2
GROUP = RING * PLANES
GROUPS = 16
CORES = 2
CHIPS = GROUPS // CORES
SEL = ROWS // GROUP
WHOLE = ROWS // (GROUP * GROUPS)
BQ = 256
BLOCKS = ROWS // BQ
SCALE = HD**-0.5 * 1.4426950408889634
NEG = -1e30
F32 = jnp.float32
BF16 = jnp.bfloat16


def iota(shape, dim):
    return lax.broadcasted_iota(jnp.int32, shape, dim)


def cols(head):
    return slice(head * HD, (head + 1) * HD)


def dot_t(a, b):
    return lax.dot_general(a, b, (((1,), (1,)), ((), ())), preferred_element_type=F32)


def dot(a, b):
    return jnp.dot(a, b, preferred_element_type=F32)


def wide(column, rows):
    return jnp.broadcast_to(column, (rows, HD))


def finish(scores, values):
    rows = scores.shape[0]
    top = jnp.max(scores, axis=1, keepdims=True)
    expo = jnp.exp2((scores - top) * SCALE)
    total = jnp.sum(expo, axis=1, keepdims=True)
    out = dot(expo.astype(BF16), values) / total
    return out, wide(top * SCALE + jnp.log2(total), rows)


def local_tile(q_ref, k_ref, vx_ref, block, head):
    low = block * BQ
    high = low + BQ
    scores = dot_t(q_ref[low:high, cols(head)], k_ref[0:high, cols(head)])
    diag = jnp.where(iota((BQ, BQ), 1) <= iota((BQ, BQ), 0), scores[:, low:], NEG)
    scores = diag if block == 0 else jnp.concatenate([scores[:, :low], diag], axis=1)
    top = jnp.max(scores, axis=1, keepdims=True)
    expo = jnp.exp2((scores - top) * SCALE)
    out = dot(expo.astype(BF16), vx_ref[0:high, head * 2 * HD : (head + 1) * 2 * HD])
    total = out[:, HD:]
    return out[:, :HD] / total, top * SCALE + jnp.log2(total)


def merge(parts):
    top = parts[0][1]
    for _, lse in parts[1:]:
        top = jnp.maximum(top, lse)
    weights = [jnp.exp2(lse - top) for _, lse in parts]
    out = sum(weight * part for weight, (part, _) in zip(weights, parts))
    total = sum(weights)
    return out / total, top + jnp.log2(total)


def three_terms(value, place):
    result = jnp.zeros(value.shape, F32)
    for term in range(3):
        head = value.astype(BF16).astype(F32)
        value = value - head
        result = jnp.where(place == term, head, result)
    return result.astype(BF16)


def pack_lse(lse):
    flat = lse.T[0:16, :]
    row = iota((16, HD), 0)
    return three_terms(jnp.where(row % 2 == 0, flat[:, :HD], flat[:, HD:]), row // 2)


def unpack_lse(packed):
    rows = packed.astype(F32)
    halves = [rows[h : h + 1] + rows[h + 2 : h + 3] + rows[h + 4 : h + 5] for h in range(2)]
    flat = jnp.concatenate(halves, axis=1)
    return jnp.broadcast_to(flat, (HD, SEL)).T


def attention_kernel(
    offg_hbm, offw_hbm, q_hbm, k_hbm, v_hbm,
    att_hbm, small_hbm,
    offg_ref, offw_ref, q_ref, k_ref, v_ref, vx, att, small, out0, lse0, out1, lse1,
    gk, gv, gq, gqr, gos, gor,
    nkv, nq, no_out, no_in,
    load, store, send, recv, wk_send, wk_recv, wq_send, wq_recv, wo_send, wo_recv,
):
    outer = lax.axis_index("outer")
    inner = lax.axis_index("inner")
    plane = inner // RING
    y = inner % RING
    chip = outer // CORES
    core = outer % CORES
    base = plane * RING
    pair = base + (y // 2) * 2 + 1 - y % 2
    across = (1 - plane) * RING + y
    reverse = base + RING - 1 - y
    diagonal = (1 - plane) * RING + RING - 1 - y
    other_core = chip * CORES + 1 - core
    mesh_id = pl.DeviceIdType.MESH

    barrier = pltpu.get_barrier_semaphore()

    def greet_inner(step, carry):
        pl.semaphore_signal(barrier, inc=1, device_id={"inner": (inner + step) % GROUP}, device_id_type=mesh_id)
        return carry

    def greet_outer(peer, carry):
        pl.semaphore_signal(barrier, inc=1, device_id={"outer": peer * CORES + core}, device_id_type=mesh_id)
        return carry

    lax.fori_loop(1, GROUP, greet_inner, 0)
    lax.fori_loop(chip + 1, CHIPS, greet_outer, 0)
    pl.semaphore_signal(barrier, inc=1, device_id={"outer": other_core}, device_id_type=mesh_id)

    loads = [
        pltpu.make_async_copy(src, dst, load.at[index])
        for index, (src, dst) in enumerate(
            ((offg_hbm, offg_ref), (offw_hbm, offw_ref), (k_hbm, k_ref), (v_hbm, v_ref), (q_hbm, q_ref))
        )
    ]
    for copy in loads:
        copy.start()
    loads[0].wait()
    loads[1].wait()

    offs1 = [offg_ref[head, outer] for head in range(HEADS)]
    offs2 = [offw_ref[head] for head in range(HEADS)]
    row8 = iota((8, HD), 0)
    offsets = jnp.where(
        row8 == 0, offs1[0], jnp.where(row8 == 1, offs1[1], jnp.where(row8 == 2, offs2[0], offs2[1]))
    )
    for head in range(HEADS):
        small[SEL + WHOLE : SEL + WHOLE + 8, cols(head)] = offsets.astype(F32)
    n1 = BQ // GROUP
    pick1 = [
        (iota((n1, BQ), 1) == iota((n1, BQ), 0) * GROUP + offs1[head]).astype(F32).astype(BF16)
        for head in range(HEADS)
    ]
    picks = []
    for block in range(BLOCKS):
        pick2 = [
            (iota((WHOLE, BQ), 1) + block * BQ == iota((WHOLE, BQ), 0) * (GROUP * GROUPS) + offs2[head])
            .astype(F32).astype(BF16)
            for head in range(HEADS)
        ]
        picks.append(jnp.concatenate(pick1 + pick2, axis=0))
    own1 = pl.multiple_of((y % 2) * SEL, SEL)
    own2 = pl.multiple_of(inner * WHOLE, WHOLE)
    own3 = pl.multiple_of(chip * WHOLE, WHOLE)
    def select(index):
        ref = (k_ref, v_ref, q_ref)[index]
        loads[2 + index].wait()
        whole = [jnp.zeros((WHOLE, HD), F32) for _ in range(HEADS)]
        for block in range(BLOCKS):
            got = dot(picks[block], ref[block * BQ : (block + 1) * BQ, :])
            for head in range(HEADS):
                rows1 = got[head * n1 : (head + 1) * n1, cols(head)].astype(BF16)
                if index == 2:
                    gq[head, block * n1 : (block + 1) * n1, :] = rows1
                else:
                    (gk, gv)[index][head, pl.ds(own1 + block * n1, n1), :] = rows1
                low = HEADS * n1 + head * WHOLE
                whole[head] += got[low : low + WHOLE, cols(head)]
        for head in range(HEADS):
            if index == 2:
                nq[pl.ds(own3, WHOLE), cols(head)] = whole[head].astype(BF16)
            else:
                nkv[core, pl.ds(own2, WHOLE), cols(index * HEADS + head)] = whole[head].astype(BF16)

    def remote(src, dst, index, axis, peer):
        return pltpu.make_async_remote_copy(
            src_ref=src, dst_ref=dst, send_sem=send.at[index], recv_sem=recv.at[index],
            device_id={axis: peer}, device_id_type=mesh_id,
        )

    def slot(index):
        return pl.ds(pl.multiple_of(index * WHOLE, WHOLE), WHOLE)

    def key_copy(peer, index):
        return pltpu.make_async_remote_copy(
            src_ref=nkv.at[core, slot(inner)], dst_ref=nkv.at[core, slot(index)],
            send_sem=wk_send.at[peer], recv_sem=wk_recv.at[index],
            device_id={"inner": peer}, device_id_type=mesh_id,
        )

    def query_copy(peer, index):
        return pltpu.make_async_remote_copy(
            src_ref=nq.at[slot(chip)], dst_ref=nq.at[slot(index)],
            send_sem=wq_send.at[peer], recv_sem=wq_recv.at[index],
            device_id={"outer": peer * CORES + core}, device_id_type=mesh_id,
        )

    def result_copy(peer, index):
        return pltpu.make_async_remote_copy(
            src_ref=no_out.at[slot(peer)], dst_ref=no_in.at[slot(index)],
            send_sem=wo_send.at[peer], recv_sem=wo_recv.at[index],
            device_id={"outer": peer * CORES + core}, device_id_type=mesh_id,
        )

    core_copy = remote(nkv.at[core], nkv.at[core], 0, "outer", other_core)
    core_in = remote(nkv.at[1 - core], nkv.at[1 - core], 0, "outer", other_core)

    def each(first, last, act):
        def body(index, carry):
            act(index)
            return carry

        lax.fori_loop(first, last, body, 0)

    def each_key(act):
        each(1, GROUP, lambda step: act((inner + step) % GROUP))

    def each_earlier(act):
        each(0, chip, act)

    def each_later(act):
        each(chip + 1, CHIPS, act)

    flows = (
        (across, plane == 1, plane == 0),
        (diagonal, plane == 1, plane == 0),
        (reverse, y >= 2, y < 2),
    )
    pair_copies = []
    query_copies = []
    result_copies = []
    for head in range(HEADS):
        place = 1 + head * 8
        rows = pl.ds(own1, SEL)
        pair_copies.append(
            [
                remote(buffer.at[head, rows], buffer.at[head, rows], place + index, "inner", pair)
                for index, buffer in enumerate((gk, gv))
            ]
        )
        query_copies.append(
            [
                remote(gq.at[head], gqr.at[head, pl.ds(flow * SEL, SEL)], place + 2 + flow, "inner", peer)
                for flow, (peer, _, _) in enumerate(flows)
            ]
        )
        result_copies.append(
            [
                remote(gos.at[head, flow], gor.at[head, flow], place + 5 + flow, "inner", peer)
                for flow, (peer, _, _) in enumerate(flows)
            ]
        )

    def ask(head):
        @pl.when(plane == 1)
        def _():
            query_copies[head][1].start()
            query_copies[head][0].start()

        @pl.when(y >= 2)
        def _():
            query_copies[head][2].start()

    select(0)
    pl.semaphore_wait(barrier, GROUP - 1 + 1 + chip)
    pair_copies[0][0].start()
    select(1)
    pair_copies[0][1].start()
    each_key(lambda peer: key_copy(peer, inner).start())
    select(2)
    ask(0)
    each_earlier(lambda peer: query_copy(peer, chip).start())
    ask(1)
    pair_copies[1][0].start()
    pair_copies[1][1].start()

    for head in range(HEADS):
        vx[:, 2 * head * HD : (2 * head + 1) * HD] = v_ref[:, cols(head)]
        vx[:, (2 * head + 1) * HD : (2 * head + 2) * HD] = jnp.ones((ROWS, HD), BF16)

    def stored(block):
        rows = pl.ds(block * BQ, BQ)
        return pltpu.make_async_copy(att.at[rows], att_hbm.at[rows], store.at[block])

    def local(block):
        for head in range(HEADS):
            c = cols(head)
            out, lse = local_tile(q_ref, k_ref, vx, block, head)
            att[block * BQ : (block + 1) * BQ, c] = out.astype(BF16)
            out0[head, block * BQ : (block + 1) * BQ, :] = out
            lse0[head, block * BQ : (block + 1) * BQ, :] = lse
        stored(block).start()

    def group_foreign(head):
        for copy in pair_copies[head]:
            copy.wait_recv()

        def serve(first, count):
            for flow in range(first, first + count):
                query_copies[head][flow].wait_recv()
            out, lse = finish(dot_t(gqr[head, first * SEL : (first + count) * SEL, :], gk[head]), gv[head])
            for index in range(count):
                rows = slice(index * SEL, (index + 1) * SEL)
                gos[head, first + index, 0:SEL, :] = out[rows].astype(BF16)
                gos[head, first + index, SEL : SEL + 16, :] = pack_lse(lse[rows])
                result_copies[head][first + index].start()

        @pl.when(plane == 0)
        def _():
            serve(1, 1)
            serve(0, 1)

        @pl.when(y < 2)
        def _():
            serve(2, 1)

    def group_own(head):
        scores = dot_t(gq[head], gk[head])
        shape = (SEL, 2 * SEL)
        out, lse = finish(jnp.where(iota(shape, 1) <= iota(shape, 0) + own1, scores, NEG), gv[head])
        out1[head] = out
        lse1[head] = lse

    def group_merge(head):
        c = cols(head)
        for flow, (_, asks, _) in enumerate(flows):

            @pl.when(asks)
            def _():
                result_copies[head][flow].wait_recv()
                here = (out1[head], lse1[head])
                there = (gor[head, flow, 0:SEL, :].astype(F32), unpack_lse(gor[head, flow, SEL : SEL + 16, :]))
                out1[head], lse1[head] = merge([here, there])

    def whole_all():
        rows = CHIPS * WHOLE
        keys = CORES * GROUP * WHOLE
        shape = (rows, keys)
        row = iota(shape, 0)
        query_pos = (row // WHOLE * CORES + core) * GROUP * WHOLE + inner * WHOLE + row % WHOLE
        allowed = iota(shape, 1) + chip * keys <= query_pos
        place = iota((rows, HD), 1) // 16
        stats = jnp.zeros((rows, HD), F32)
        for head in range(HEADS):
            key_rows = nkv[:, :, cols(head)].reshape(keys, HD)
            value_rows = nkv[:, :, cols(HEADS + head)].reshape(keys, HD)
            out, lse = finish(jnp.where(allowed, dot_t(nq[:, cols(head)], key_rows), NEG), value_rows)
            no_out[:, cols(head)] = out.astype(BF16)
            stats = stats + three_terms(lse, place - 3 * head).astype(F32)
        no_out[:, cols(HEADS)] = stats.astype(BF16)
        no_in[slot(chip), :] = no_out[slot(chip), :]

    def whole_merge():
        each_earlier(lambda peer: result_copy(peer, peer).wait_recv())
        stats = no_in[:, cols(HEADS)].astype(F32)
        known = iota((CHIPS, WHOLE, HD), 0) <= chip
        merged = []
        for head in range(HEADS):
            parts = jnp.where(known, no_in[:, cols(head)].astype(F32).reshape(CHIPS, WHOLE, HD), 0.0)
            lane = 48 * head
            lse = stats[:, lane : lane + 1] + stats[:, lane + 16 : lane + 17] + stats[:, lane + 32 : lane + 33]
            lse = jnp.where(known, wide(lse, CHIPS * WHOLE).reshape(CHIPS, WHOLE, HD), NEG)
            top = jnp.max(lse, axis=0)
            weight = jnp.exp2(lse - top[None])
            total = jnp.sum(weight, axis=0)
            merged.append((jnp.sum(weight * parts, axis=0) / total, top + jnp.log2(total)))
        return merged

    def last_merge(head, whole):
        c = cols(head)
        group = (out1[head], lse1[head])
        rows = pl.ds(offs1[head], SEL, stride=GROUP)
        small[0:SEL, c] = merge([(out0[head, rows, :], lse0[head, rows, :]), group])[0]
        rows = pl.ds(offs2[head], WHOLE, stride=GROUP * GROUPS)
        rows1 = pl.ds(offs2[head] // GROUP, WHOLE, stride=GROUPS)
        same = jnp.full((WHOLE, HD), offs2[head] % GROUP) == offs1[head]
        lse = jnp.where(same, lse1[head, rows1, :], NEG)
        parts = [(out0[head, rows, :], lse0[head, rows, :]), (out1[head, rows1, :], lse), whole[head]]
        small[SEL : SEL + WHOLE, c] = merge(parts)[0]

    local(7)
    local(6)
    each_key(lambda peer: key_copy(peer, peer).wait_recv())
    core_copy.start()
    local(5)
    group_foreign(0)
    local(4)
    core_in.wait_recv()
    each_later(lambda peer: query_copy(peer, peer).wait_recv())
    whole_all()
    each_later(lambda peer: result_copy(peer, chip).start())
    group_foreign(1)
    group_own(0)
    group_own(1)
    local(3)
    local(2)
    local(1)
    local(0)
    whole = whole_merge()
    for head in range(HEADS):
        group_merge(head)
        last_merge(head, whole)
    last = pltpu.make_async_copy(small, small_hbm, store.at[BLOCKS])
    last.start()

    each_key(lambda peer: key_copy(peer, inner).wait_send())
    each_earlier(lambda peer: query_copy(peer, chip).wait_send())
    each_later(lambda peer: result_copy(peer, chip).wait_send())
    for block in range(BLOCKS):
        stored(block).wait()
    last.wait()
    core_copy.wait_send()
    for head in range(HEADS):
        for copy in pair_copies[head]:
            copy.wait_send()
        for flow, (_, asks, serves) in enumerate(flows):

            @pl.when(asks)
            def _():
                query_copies[head][flow].wait_send()

            @pl.when(serves)
            def _():
                result_copies[head][flow].wait_send()


SMALL = (SEL + WHOLE + 8, HEADS * HD)


def attention(queries, keys, values, offsets_group, offsets_global):
    hbm = pl.BlockSpec(memory_space=pltpu.HBM)
    dma = pltpu.SemaphoreType.DMA
    width = HEADS * HD
    return pl.pallas_call(
        attention_kernel,
        out_shape=[
            jax.ShapeDtypeStruct((ROWS, width), BF16),
            jax.ShapeDtypeStruct(SMALL, F32),
        ],
        in_specs=[hbm] * 5,
        out_specs=[hbm] * 2,
        scratch_shapes=[
            pltpu.SMEM((HEADS, GROUPS), jnp.int32),
            pltpu.SMEM((HEADS,), jnp.int32),
            pltpu.VMEM((ROWS, width), BF16),
            pltpu.VMEM((ROWS, width), BF16),
            pltpu.VMEM((ROWS, width), BF16),
            pltpu.VMEM((ROWS, 2 * width), BF16),
            pltpu.VMEM((ROWS, width), BF16),
            pltpu.VMEM(SMALL, F32),
            pltpu.VMEM((HEADS, ROWS, HD), F32),
            pltpu.VMEM((HEADS, ROWS, HD), F32),
            pltpu.VMEM((HEADS, SEL, HD), F32),
            pltpu.VMEM((HEADS, SEL, HD), F32),
            pltpu.VMEM((HEADS, 2 * SEL, HD), BF16),
            pltpu.VMEM((HEADS, 2 * SEL, HD), BF16),
            pltpu.VMEM((HEADS, SEL, HD), BF16),
            pltpu.VMEM((HEADS, 3 * SEL, HD), BF16),
            pltpu.VMEM((HEADS, 3, SEL + 16, HD), BF16),
            pltpu.VMEM((HEADS, 3, SEL + 16, HD), BF16),
            pltpu.VMEM((CORES, GROUP * WHOLE, 2 * width), BF16),
            pltpu.VMEM((CHIPS * WHOLE, width), BF16),
            pltpu.VMEM((CHIPS * WHOLE, width + HD), BF16),
            pltpu.VMEM((CHIPS * WHOLE, width + HD), BF16),
            dma((5,)),
            dma((BLOCKS + 1,)),
            dma((17,)),
            dma((17,)),
            dma((GROUP,)),
            dma((GROUP,)),
            dma((CHIPS,)),
            dma((CHIPS,)),
            dma((CHIPS,)),
            dma((CHIPS,)),
        ],
        compiler_params=pltpu.CompilerParams(
            collective_id=0, has_side_effects=True, vmem_limit_bytes=56 * 2**20
        ),
        cost_estimate=pl.CostEstimate(flops=5 * 10**9, bytes_accessed=4 * 2**20, transcendentals=6 * 10**6),
        name="attention",
    )(offsets_group.T, offsets_global, queries, keys, values)


SLOTS = 4


def project_kernel(att_hbm, small_hbm, w_hbm, o_ref, att, small, w_ref, buf, load, sem):
    def copy(block):
        return pltpu.make_async_copy(
            buf.at[block % SLOTS], o_ref.at[pl.ds(block * BQ, BQ)], sem.at[block % SLOTS]
        )

    def load_block(block):
        rows = pl.ds(block * BQ, BQ)
        return pltpu.make_async_copy(att_hbm.at[rows], att.at[rows], load.at[2 + block])

    w_copy = pltpu.make_async_copy(w_hbm, w_ref, load.at[1])
    small_copy = pltpu.make_async_copy(small_hbm, small, load.at[0])
    small_copy.start()
    load_block(0).start()
    w_copy.start()
    for block in range(1, BLOCKS):
        load_block(block).start()
    small_copy.wait()

    n1 = BQ // GROUP
    n2 = BQ // (GROUP * GROUPS)
    width = HEADS * HD
    spots = iota((BQ, width), 0)
    low = SEL + WHOLE
    left = iota((1, width), 1) < HD
    offset1 = jnp.where(left, small[low : low + 1, :], small[low + 1 : low + 2, :]).astype(jnp.int32)
    offset2 = jnp.where(left, small[low + 2 : low + 3, :], small[low + 3 : low + 4, :]).astype(jnp.int32)

    def spread(first, count):
        part = small[first : first + count, :]
        return jnp.broadcast_to(part[:, None, :], (count, BQ // count, width)).reshape(BQ, width)

    for block in range(BLOCKS):
        rows = slice(block * BQ, (block + 1) * BQ)
        load_block(block).wait()
        merged = jnp.where(spots % GROUP == offset1, spread(block * n1, n1), att[rows, :].astype(F32))
        merged = jnp.where(spots % (GROUP * GROUPS) == offset2, spread(SEL + block * n2, n2), merged).astype(BF16)
        if block == 0:
            w_copy.wait()
        if block >= SLOTS:
            copy(block - SLOTS).wait()
        buf[block % SLOTS] = dot(merged, w_ref[...]).astype(BF16)
        copy(block).start()
    for block in range(BLOCKS - SLOTS, BLOCKS):
        copy(block).wait()


def project(parts, weight):
    hbm = pl.BlockSpec(memory_space=pltpu.HBM)
    width = weight.shape[1]
    return pl.pallas_call(
        project_kernel,
        out_shape=jax.ShapeDtypeStruct((ROWS, width), BF16),
        in_specs=[hbm] * 3,
        out_specs=hbm,
        scratch_shapes=[
            pltpu.VMEM((ROWS, HEADS * HD), BF16),
            pltpu.VMEM(SMALL, F32),
            pltpu.VMEM((HEADS * HD, width), BF16),
            pltpu.VMEM((SLOTS, BQ, width), BF16),
            pltpu.SemaphoreType.DMA((2 + BLOCKS,)),
            pltpu.SemaphoreType.DMA((SLOTS,)),
        ],
        compiler_params=pltpu.CompilerParams(vmem_limit_bytes=56 * 2**20),
        cost_estimate=pl.CostEstimate(flops=43 * 10**8, bytes_accessed=19 * 2**20, transcendentals=0),
        name="project",
    )(*parts, weight)


def per_device(queries, keys, values, offsets_group, offsets_global, out_weight):
    return project(attention(queries, keys, values, offsets_group, offsets_global), out_weight)


def solution(mesh):
    rows = P(("outer", "inner"), None)
    return jax.shard_map(
        per_device, mesh=mesh, in_specs=(rows, rows, rows, P(), P(), P()), out_specs=rows, check_vma=False
    )
```

time: 217 us -> 34.7 us (0.16); the launches traced: 212 us -> 34.3 us
  blocking collectives: 60.3 us -> 0 us
  matrix products: 43.1 us -> 0 us
  local copies, waits for them, and re-layouts: 38.2 us -> 0 us
  Pallas kernels: 0 us -> 34.1 us
  waiting for transfers between devices: 29.4 us -> 0 us
  between operations: 21.1 us -> 0.17 us
  other arithmetic: 20.1 us -> 0 us
    all_gather x2 -> x0, blocking collectives: 60.3 us -> none  [the longest x1 30.2 us: per_device(): lax.all_gather(sel_k, 'inner', axis=0, tiled=True)]
    dot_general x25 -> x0, matrix products: 43.1 us -> none  [the longest x12 18.3 us: attend(): jnp.dot(expo.astype(jnp.bfloat16), values_in, preferred_element_type=jnp....]
    pallas_call x0 -> x2, Pallas kernels: none -> 34.1 us  [the longest x1 24.9 us: attention(): pl.pallas_call(attention_kernel, out_shape=[jax.ShapeDtypeStruct((ROWS, w...]
    all_gather x4 -> x0, waiting for transfers between devices: 29.4 us -> none  [the longest x1 29.3 us: per_device(): lax.all_gather(part_v, 'outer', axis=0, tiled=True)]
    dynamic_update_slice x8 -> x0, local copies, waits for them, and re-layouts: 10.2 us -> none  [the longest x4 9.05 us: blend(): acc3 = lax.dynamic_update_index_in_dim(acc3, mixed, offset, 1)]
    dynamic_slice x12 -> x0, local copies, waits for them, and re-layouts: 10.2 us -> none  [the longest x7 8.23 us: select_rows(): lax.dynamic_index_in_dim(part.reshape(rows // rate, rate, HD), offset, 1,...]
    slice x5 -> x0, local copies, waits for them, and re-layouts: 7.77 us -> none  [the longest x3 6.59 us: per_device(): acc, lse = local_pattern(queries[:, cols], keys[:, cols], values[:, cols])]
    reduce_sum x12 -> x0, other arithmetic: 6.96 us -> none  [attend(): denom = jnp.sum(expo, axis=1)]
  transfers between devices with their start and end apart: 4 -> 0, of which waited for: 1 -> 0; matrix products, arithmetic and copies ran while one was open for 34% -> 0% of each run, Pallas kernels for 0% -> 0%
where the time goes in v2:
time: 34.7 us; the launch traced here: 34.3 us
  Pallas kernels  34.1 us (98%)
    pallas_call x1, Pallas kernels, attention(): pl.pallas_call(attention_kernel, out_shape=[jax.ShapeDtypeStruct((ROWS, w...  24.9 us
    pallas_call x1, Pallas kernels, project(): pl.pallas_call(project_kernel, out_shape=jax.ShapeDtypeStruct((ROWS, widt...  9.26 us

profile of v2, /device:TPU:38, one launch (start us, length us, event | category | flops | bytes accessed | tf_op | source)
XLA Modules:
  0.0 34.3 jit_solution(9608311389691457776)
XLA Ops:
  0.0 24.9 %attention.1 = (bf16[2048,256]{1,0:T(8,128)(2,1)}, f32[280,256]{1,0:T(8,128)}) custom-call(s32[2,16]{1,0:T(2,128)} %bitcast.1, s32[2]{0:T(128)} %offw_hbm.1, bf16[2048,256]{1,0:T(8,128)(2,1)} %q_hbm.1, bf16[2048,256]{1,0:T(8,128)(2,1)} %k_hbm.1, bf16[2048,256]{1,0:T(8,128)(2,1)} %v_hbm.1), custom_call_target="tpu_custom_call" | custom-call | flops 5000000000 | bytes 4194304 | tf_op jit(solution)/shard_map/attention/pallas_call | solution.py:453
  24.9 9.3 %project.1 = bf16[2048,4096]{1,0:T(8,128)(2,1)} custom-call(bf16[2048,256]{1,0:T(8,128)(2,1)} %get-tuple-element.7.att_hbm, f32[280,256]{1,0:T(8,128)} %get-tuple-element.8.small_hbm, bf16[256,4096]{1,0:T(8,128)(2,1)} %w_hbm.1), custom_call_target="tpu_custom_call" | custom-call | flops 4300000256 | bytes 19922944 | tf_op jit(solution)/shard_map/project/pallas_call | solution.py:556

commit v3 on v2

--- a/solution.py
+++ b/solution.py
@@ -281,17 +281,14 @@
             query_copies[head][2].start()
 
     select(0)
+    select(1)
     pl.semaphore_wait(barrier, GROUP - 1 + 1 + chip)
+    each_key(lambda peer: key_copy(peer, inner).start())
     pair_copies[0][0].start()
-    select(1)
     pair_copies[0][1].start()
-    each_key(lambda peer: key_copy(peer, inner).start())
     select(2)
     ask(0)
     each_earlier(lambda peer: query_copy(peer, chip).start())
-    ask(1)
-    pair_copies[1][0].start()
-    pair_copies[1][1].start()
 
     for head in range(HEADS):
         vx[:, 2 * head * HD : (2 * head + 1) * HD] = v_ref[:, cols(head)]
@@ -311,9 +308,6 @@
         stored(block).start()
 
     def group_foreign(head):
-        for copy in pair_copies[head]:
-            copy.wait_recv()
-
         def serve(first, count):
             for flow in range(first, first + count):
                 query_copies[head][flow].wait_recv()
@@ -332,6 +326,10 @@
         @pl.when(y < 2)
         def _():
             serve(2, 1)
+
+    def pair_wait(head):
+        for copy in pair_copies[head]:
+            copy.wait_recv()
 
     def group_own(head):
         scores = dot_t(gq[head], gk[head])
@@ -399,19 +397,24 @@
 
     local(7)
     local(6)
+    ask(1)
+    pair_copies[1][0].start()
+    pair_copies[1][1].start()
+    local(5)
+    local(4)
     each_key(lambda peer: key_copy(peer, peer).wait_recv())
     core_copy.start()
-    local(5)
+    pair_wait(0)
+    group_own(0)
     group_foreign(0)
-    local(4)
+    local(3)
     core_in.wait_recv()
     each_later(lambda peer: query_copy(peer, peer).wait_recv())
     whole_all()
     each_later(lambda peer: result_copy(peer, chip).start())
+    pair_wait(1)
     group_foreign(1)
-    group_own(0)
     group_own(1)
-    local(3)
     local(2)
     local(1)
     local(0)

time: 34.7 us -> 32.6 us (0.939)
  Pallas kernels: 34.1 us -> 32.3 us
    pallas_call x1, Pallas kernels: 24.9 us -> 23 us  [attention(): pl.pallas_call(attention_kernel, out_shape=[jax.ShapeDtypeStruct((ROWS, w...]
where the time goes in v3:
time: 32.6 us; the launch traced here: 32.4 us
  Pallas kernels  32.3 us (99%)
    pallas_call x1, Pallas kernels, attention(): pl.pallas_call(attention_kernel, out_shape=[jax.ShapeDtypeStruct((ROWS, w...  23 us
    pallas_call x1, Pallas kernels, project(): pl.pallas_call(project_kernel, out_shape=jax.ShapeDtypeStruct((ROWS, widt...  9.27 us

profile of v3, /device:TPU:38, one launch (start us, length us, event | category | flops | bytes accessed | tf_op | source)
XLA Modules:
  0.0 32.4 jit_solution(10355404200370848830)
XLA Ops:
  0.0 23.0 %attention.1 = (bf16[2048,256]{1,0:T(8,128)(2,1)}, f32[280,256]{1,0:T(8,128)}) custom-call(s32[2,16]{1,0:T(2,128)} %bitcast.1, s32[2]{0:T(128)} %offw_hbm.1, bf16[2048,256]{1,0:T(8,128)(2,1)} %q_hbm.1, bf16[2048,256]{1,0:T(8,128)(2,1)} %k_hbm.1, bf16[2048,256]{1,0:T(8,128)(2,1)} %v_hbm.1), custom_call_target="tpu_custom_call" | custom-call | flops 5000000000 | bytes 4194304 | tf_op jit(solution)/shard_map/attention/pallas_call | solution.py:456
  23.0 9.3 %project.1 = bf16[2048,4096]{1,0:T(8,128)(2,1)} custom-call(bf16[2048,256]{1,0:T(8,128)(2,1)} %get-tuple-element.7.att_hbm, f32[280,256]{1,0:T(8,128)} %get-tuple-element.8.small_hbm, bf16[256,4096]{1,0:T(8,128)(2,1)} %w_hbm.1), custom_call_target="tpu_custom_call" | custom-call | flops 4300000256 | bytes 19922944 | tf_op jit(solution)/shard_map/project/pallas_call | solution.py:559

commit v4 on v3

--- a/solution.py
+++ b/solution.py
@@ -401,17 +401,17 @@
     pair_copies[1][0].start()
     pair_copies[1][1].start()
     local(5)
-    local(4)
     each_key(lambda peer: key_copy(peer, peer).wait_recv())
     core_copy.start()
     pair_wait(0)
     group_own(0)
     group_foreign(0)
-    local(3)
     core_in.wait_recv()
     each_later(lambda peer: query_copy(peer, peer).wait_recv())
     whole_all()
     each_later(lambda peer: result_copy(peer, chip).start())
+    local(4)
+    local(3)
     pair_wait(1)
     group_foreign(1)
     group_own(1)
@@ -516,18 +516,23 @@
         rows = pl.ds(block * BQ, BQ)
         return pltpu.make_async_copy(att_hbm.at[rows], att.at[rows], load.at[2 + block])
 
-    w_copy = pltpu.make_async_copy(w_hbm, w_ref, load.at[1])
+    width = HEADS * HD
+    halves = [slice(part * w_ref.shape[1] // 2, (part + 1) * w_ref.shape[1] // 2) for part in range(2)]
+    w_copies = [
+        pltpu.make_async_copy(w_hbm.at[:, half], w_ref.at[:, half], load.at[1 + BLOCKS * part + part])
+        for part, half in enumerate(halves)
+    ]
     small_copy = pltpu.make_async_copy(small_hbm, small, load.at[0])
     small_copy.start()
     load_block(0).start()
-    w_copy.start()
+    for item in w_copies:
+        item.start()
     for block in range(1, BLOCKS):
         load_block(block).start()
     small_copy.wait()
 
     n1 = BQ // GROUP
     n2 = BQ // (GROUP * GROUPS)
-    width = HEADS * HD
     spots = iota((BQ, width), 0)
     low = SEL + WHOLE
     left = iota((1, width), 1) < HD
@@ -544,10 +549,13 @@
         merged = jnp.where(spots % GROUP == offset1, spread(block * n1, n1), att[rows, :].astype(F32))
         merged = jnp.where(spots % (GROUP * GROUPS) == offset2, spread(SEL + block * n2, n2), merged).astype(BF16)
         if block == 0:
-            w_copy.wait()
-        if block >= SLOTS:
-            copy(block - SLOTS).wait()
-        buf[block % SLOTS] = dot(merged, w_ref[...]).astype(BF16)
+            for item, half in zip(w_copies, halves):
+                item.wait()
+                buf[0, :, half] = dot(merged, w_ref[:, half]).astype(BF16)
+        else:
+            if block >= SLOTS:
+                copy(block - SLOTS).wait()
+            buf[block % SLOTS] = dot(merged, w_ref[...]).astype(BF16)
         copy(block).start()
     for block in range(BLOCKS - SLOTS, BLOCKS):
         copy(block).wait()
@@ -566,7 +574,7 @@
             pltpu.VMEM(SMALL, F32),
             pltpu.VMEM((HEADS * HD, width), BF16),
             pltpu.VMEM((SLOTS, BQ, width), BF16),
-            pltpu.SemaphoreType.DMA((2 + BLOCKS,)),
+            pltpu.SemaphoreType.DMA((3 + BLOCKS,)),
             pltpu.SemaphoreType.DMA((SLOTS,)),
         ],
         compiler_params=pltpu.CompilerParams(vmem_limit_bytes=56 * 2**20),

time: 32.6 us -> 31.6 us (0.969)
  Pallas kernels: 32.3 us -> 31.3 us
    pallas_call x1, Pallas kernels: 23 us -> 22.3 us  [attention(): pl.pallas_call(attention_kernel, out_shape=[jax.ShapeDtypeStruct((ROWS, w...]
where the time goes in v4:
time: 31.6 us; the launch traced here: 31.5 us
  Pallas kernels  31.3 us (99%)
    pallas_call x1, Pallas kernels, attention(): pl.pallas_call(attention_kernel, out_shape=[jax.ShapeDtypeStruct((ROWS, w...  22.3 us
    pallas_call x1, Pallas kernels, project(): pl.pallas_call(project_kernel, out_shape=jax.ShapeDtypeStruct((ROWS, widt...  9.04 us

profile of v4, /device:TPU:38, one launch (start us, length us, event | category | flops | bytes accessed | tf_op | source)
XLA Modules:
  0.0 31.5 jit_solution(12998188866800763266)
XLA Ops:
  0.0 22.3 %attention.1 = (bf16[2048,256]{1,0:T(8,128)(2,1)}, f32[280,256]{1,0:T(8,128)}) custom-call(s32[2,16]{1,0:T(2,128)} %bitcast.1, s32[2]{0:T(128)} %offw_hbm.1, bf16[2048,256]{1,0:T(8,128)(2,1)} %q_hbm.1, bf16[2048,256]{1,0:T(8,128)(2,1)} %k_hbm.1, bf16[2048,256]{1,0:T(8,128)(2,1)} %v_hbm.1), custom_call_target="tpu_custom_call" | custom-call | flops 5000000000 | bytes 4194304 | tf_op jit(solution)/shard_map/attention/pallas_call | solution.py:456
  22.3 9.0 %project.1 = bf16[2048,4096]{1,0:T(8,128)(2,1)} custom-call(bf16[2048,256]{1,0:T(8,128)(2,1)} %get-tuple-element.7.att_hbm, f32[280,256]{1,0:T(8,128)} %get-tuple-element.8.small_hbm, bf16[256,4096]{1,0:T(8,128)(2,1)} %w_hbm.1), custom_call_target="tpu_custom_call" | custom-call | flops 4300000256 | bytes 19922944 | tf_op jit(solution)/shard_map/project/pallas_call | solution.py:567

commit v5 on v4

--- a/solution.py
+++ b/solution.py
@@ -411,9 +411,9 @@
     whole_all()
     each_later(lambda peer: result_copy(peer, chip).start())
     local(4)
-    local(3)
     pair_wait(1)
     group_foreign(1)
+    local(3)
     group_own(1)
     local(2)
     local(1)

time: 31.6 us -> 31.3 us (level)
  no operation moved by 1% of the time
where the time goes in v5:
time: 31.3 us; the launch traced here: 31.2 us
  Pallas kernels  31.1 us (99%)
    pallas_call x1, Pallas kernels, attention(): pl.pallas_call(attention_kernel, out_shape=[jax.ShapeDtypeStruct((ROWS, w...  22 us
    pallas_call x1, Pallas kernels, project(): pl.pallas_call(project_kernel, out_shape=jax.ShapeDtypeStruct((ROWS, widt...  9.05 us

profile of v5, /device:TPU:38, one launch (start us, length us, event | category | flops | bytes accessed | tf_op | source)
XLA Modules:
  0.0 31.2 jit_solution(17790528656776746008)
XLA Ops:
  0.0 22.0 %attention.1 = (bf16[2048,256]{1,0:T(8,128)(2,1)}, f32[280,256]{1,0:T(8,128)}) custom-call(s32[2,16]{1,0:T(2,128)} %bitcast.1, s32[2]{0:T(128)} %offw_hbm.1, bf16[2048,256]{1,0:T(8,128)(2,1)} %q_hbm.1, bf16[2048,256]{1,0:T(8,128)(2,1)} %k_hbm.1, bf16[2048,256]{1,0:T(8,128)(2,1)} %v_hbm.1), custom_call_target="tpu_custom_call" | custom-call | flops 5000000000 | bytes 4194304 | tf_op jit(solution)/shard_map/attention/pallas_call | solution.py:456
  22.0 9.0 %project.1 = bf16[2048,4096]{1,0:T(8,128)(2,1)} custom-call(bf16[2048,256]{1,0:T(8,128)(2,1)} %get-tuple-element.7.att_hbm, f32[280,256]{1,0:T(8,128)} %get-tuple-element.8.small_hbm, bf16[256,4096]{1,0:T(8,128)(2,1)} %w_hbm.1), custom_call_target="tpu_custom_call" | custom-call | flops 4300000256 | bytes 19922944 | tf_op jit(solution)/shard_map/project/pallas_call | solution.py:567
